TPU v7x, 128 devices: a whole 4x4x4 slice. The times are simulated.
128 devices in a mesh: grp: 8 (over y, x_lo), sub: 16 (over x_hi, z, core).
Axes of the slice: x: 4 (x_hi: 2, x_lo: 2; x = x_hi * 2 + x_lo), y: 4, z: 4, core: 2. Of those that a mesh axis runs over, the one named last changes fastest.
Arguments:
- records: bfloat16 [4096, 2, 2048], P(('grp', 'sub')), may hold values from -6 to 6
- ref_bin: int32 [8, 512, 16, 256], P('grp', None, 'sub'), may hold values from 0 to 63
- ref_table: bfloat16 [64, 8], replicated
Outputs:
- adjoint: float32 [4096, 2, 2048], P(('grp', 'sub'))
All inputs are finite; a program needn't handle non-finite values.
Results may differ from a plain program's by a relative error of at most 0.007.
Values may be sent and summed in bfloat16 or wider, within the bound.
A program may use at most 128 MiB of HBM per device.

v0:
```python
import math

import jax
import jax.numpy as jnp
from jax import lax
from jax.sharding import PartitionSpec as P

BANDS = 4


def band_split(panel):
    count = panel.shape[0]
    return (panel[:, 0].reshape(count, BANDS, -1), panel[:, 1].reshape(count, BANDS, -1))


def cross(left, right):
    return jnp.einsum("rbf,kbf->rbk", left, right, preferred_element_type=jnp.float32)


def toward_columns(left, right):
    return jnp.einsum("rbk,kbf->rbf", left, right, preferred_element_type=jnp.float32)


def double_sided(
    residual_real_part,
    residual_imaginary,
    mirrored_real,
    mirrored_imaginary,
    column_real_part,
    column_imaginary,
    frequency_grid,
):

    def full_term(start, count):
        part_re = (
            toward_columns(residual_real_part, column_real_part)
            - toward_columns(residual_imaginary, column_imaginary)
            + toward_columns(mirrored_real, column_real_part)
            + toward_columns(mirrored_imaginary, column_imaginary)
        )
        part_im = (
            toward_columns(residual_real_part, column_imaginary)
            + toward_columns(residual_imaginary, column_real_part)
            + toward_columns(mirrored_real, column_imaginary)
            - toward_columns(mirrored_imaginary, column_real_part)
        )
        return jnp.stack((part_re, part_im), axis=1).reshape(count, 2, frequency_grid)

    return full_term


def per_device(records, ref_bin, ref_table):
    per_dev = records.shape[0]
    frequency_grid = records.shape[2]
    n_grp = lax.axis_size("grp")
    n_sub = lax.axis_size("sub")
    stations = per_dev * n_grp * n_sub
    scale = 1.0 / math.sqrt(frequency_grid // BANDS)
    rows_panel = lax.all_gather(records, "sub", axis=0, tiled=True)
    cols_panel = lax.all_gather(records, "grp", axis=0, tiled=True)
    row_count = rows_panel.shape[0]
    col_count = cols_panel.shape[0]
    row_real, row_imag = band_split(rows_panel)
    column_real_part, column_imaginary = band_split(cols_panel)
    corr_real = (cross(row_real, column_real_part) + cross(row_imag, column_imaginary)) * scale
    corr_imag = (cross(row_imag, column_real_part) - cross(row_real, column_imaginary)) * scale
    levels = jnp.arange(ref_table.shape[0], dtype=jnp.int32)

    def lookup(block_ids):
        onehot = (block_ids[:, :, None] == levels[None, None, :]).astype(jnp.bfloat16)
        return jnp.einsum("rkn,nj->rjk", onehot, ref_table, preferred_element_type=jnp.float32)

    bin_tile = ref_bin.reshape(row_count, col_count)
    looked = lax.map(lookup, bin_tile.reshape(8, row_count // 8, col_count)).reshape(
        row_count, 2 * BANDS, col_count
    )
    residual_real_part = (corr_real - looked[:, :BANDS]).astype(jnp.bfloat16)
    residual_imaginary = (corr_imag - looked[:, BANDS:]).astype(jnp.bfloat16)
    stacked = jnp.stack((residual_real_part, residual_imaginary), axis=1)
    blocks = stacked.reshape(n_sub, per_dev, 2, BANDS, n_grp, per_dev)
    blocks = jnp.transpose(blocks, (4, 0, 5, 2, 3, 1)).reshape(
        n_grp * n_sub, per_dev, 2 * BANDS * per_dev
    )
    received = lax.all_to_all(blocks, ("grp", "sub"), split_axis=0, concat_axis=0, tiled=True)
    received = received.reshape(n_grp, n_sub, per_dev, 2, BANDS, per_dev)
    received = jnp.transpose(received, (1, 2, 3, 4, 0, 5)).reshape(row_count, 2, BANDS, col_count)
    full_term = double_sided(
        residual_real_part,
        residual_imaginary,
        received[:, 0],
        received[:, 1],
        column_real_part,
        column_imaginary,
        frequency_grid,
    )
    summed = lax.psum_scatter(
        full_term(jnp.int32(0), per_dev * lax.axis_size("sub")),
        "sub",
        scatter_dimension=0,
        tiled=True,
    )
    return summed / math.sqrt(stations)


def solution(mesh):
    in_specs = (P(("grp", "sub"), None, None), P("grp", None, "sub", None), P())
    out_specs = P(("grp", "sub"), None, None)
    return jax.shard_map(
        per_device, mesh=mesh, in_specs=in_specs, out_specs=out_specs, check_vma=False
    )
```

profile of v0, /device:TPU:1, one launch (start us, length us, event | category | flops | bytes accessed | tf_op | source)
XLA Modules:
  0.0 491.2 jit_solution(9496337264461428607)
XLA Ops:
  9.1 17.8 %while.11 = (s32[]{:T(128)}, f32[8,64,8,256]{3,2,1,0:T(8,128)}, s32[8,64,256]{2,1,0:T(8,128)S(1)}, bf16[64,8]{0,1:T(8,128)(2,1)}, s32[]{:T(128)}) while((s32[]{:T(128)}, f32[8,64,8,256]{3,2,1,0:T(8,128)}, s32[8,64,256]{2,1,0:T(8,128)S(1)}, bf16[64,8]{0,1:T(8,128)(2,1)}, s32[]{:T(128)}) %tuple.33), condition=%wide.region_1.2_spmd.clone, body=%wide.region_0.1_spmd.clone.sunk | while | flops 17825792 | bytes 723521 | solution.py:74
  26.9 5.6 %fusion.13 = (f32[512,4,256]{2,1,0:T(4,128)}, f32[512,4,256]{2,1,0:T(4,128)S(1)}) fusion(f32[512,8,256]{2,1,0:T(8,128)} %bitcast.96), kind=kLoop, calls=%fused_computation.23 | loop fusion | bytes 8388608 | tf_op jit(solution)/shard_map/slice | solution.py:77
  37.4 26.7 %all-gather.3.cloned.1.call-done = bf16[256,2,2048]{2,1,0:T(2,128)(2,1)} async-done(((bf16[32,2,2048]{2,1,0:T(2,128)(2,1)}), bf16[256,2,2048]{2,1,0:T(2,128)(2,1)}) %all-gather.3.cloned.1.call-update) | async-done | bytes 2097168 | tf_op jit(solution)/shard_map/all_gather | solution.py:60
  64.1 6.5 %fusion.15 = (bf16[256,1,2048]{2,1,0:T(2,128)(2,1)}, bf16[256,1,2048]{2,1,0:T(2,128)(2,1)S(1)}) fusion(bf16[256,2,2048]{2,1,0:T(2,128)(2,1)} %all-gather.3.cloned.1.call-done), kind=kLoop, calls=%fused_computation.25 | loop fusion | bytes 4194304 | tf_op jit(solution)/shard_map/slice | solution.py:13
  72.5 4.5 copy.78
  77.0 45.0 %all-gather.5.cloned.1.call-done = bf16[512,2,2048]{2,1,0:T(2,128)(2,1)} async-done(((bf16[32,2,2048]{2,1,0:T(2,128)(2,1)}), bf16[512,2,2048]{2,1,0:T(2,128)(2,1)}) %all-gather.5.cloned.1.call-update) | async-done | bytes 4194320 | tf_op jit(solution)/shard_map/all_gather | solution.py:59
  122.0 10.2 %fusion.14 = (bf16[512,1,2048]{2,1,0:T(2,128)(2,1)}, bf16[512,1,2048]{2,1,0:T(2,128)(2,1)}) fusion(bf16[512,2,2048]{2,1,0:T(2,128)(2,1)} %all-gather.5.cloned.1.call-done), kind=kLoop, calls=%fused_computation.24 | loop fusion | bytes 8388608 | tf_op jit(solution)/shard_map/slice | solution.py:13
  132.1 10.5 %copy.77 = bf16[512,1,2048]{0,2,1:T(8,128)(2,1)} copy(bf16[512,1,2048]{2,1,0:T(2,128)(2,1)} %get-tuple-element.53) | data formatting | bytes 4194304
  142.6 10.5 %copy.79 = bf16[512,1,2048]{0,2,1:T(8,128)(2,1)} copy(bf16[512,1,2048]{2,1,0:T(2,128)(2,1)} %get-tuple-element.54) | data formatting | bytes 4194304
  162.4 7.6 %copy.56 = bf16[16,32,1,4,8,32]{1,3,2,5,0,4:T(4,128)(2,1)} copy(bf16[16,32,1,4,8,32]{1,0,5,4,3,2:T(8,128)(2,1)} %stack.18) | data formatting | bytes 2097152 | tf_op jit(solution)/shard_map/stack | solution.py:79
  174.8 5.6 %copy.57 = bf16[16,32,1,4,8,32]{1,3,2,5,0,4:T(4,128)(2,1)S(1)} copy(bf16[16,32,1,4,8,32]{1,0,5,4,3,2:T(8,128)(2,1)} %stack.19) | data formatting | bytes 2097152 | tf_op jit(solution)/shard_map/stack | solution.py:79
  180.4 8.3 %maximum_bitcast_fusion = bf16[8,16,32,2,4,32]{5,4,3,2,1,0:T(4,128)(2,1)} fusion(bf16[16,32,1,4,8,32]{1,3,2,5,0,4:T(4,128)(2,1)S(1)} %copy.57, bf16[16,32,1,4,8,32]{1,3,2,5,0,4:T(4,128)(2,1)S(1)} %copy-done.4), kind=kLoop, calls=%fused_computation.8 | loop fusion | flops 1048576 | bytes 4194304 | tf_op jit(solution)/shard_map/transpose | solution.py:81
  188.7 12.5 %reshape.26 = bf16[128,32,256]{2,1,0:T(8,128)(2,1)} reshape(bf16[8,16,32,2,4,32]{5,4,3,2,1,0:T(4,128)(2,1)} %maximum_bitcast_fusion) | data formatting | bytes 4194304 | tf_op jit(solution)/shard_map/reshape | solution.py:81
  201.2 6.1 %all-to-all-start = ((bf16[128,32,256]{2,1,0:T(8,128)(2,1)}), bf16[128,32,256]{2,1,0:T(8,128)(2,1)}, u32[]{:S(2)}, u32[]{:S(2)}) async-start(bf16[128,32,256]{2,1,0:T(8,128)(2,1)} %reshape.26), calls=%async_computation | async-start | bytes 4194304 | tf_op jit(solution)/shard_map/all_to_all | solution.py:84
  207.3 4.0 fusion.18
  214.0 22.6 %all-to-all-done = bf16[128,32,256]{2,1,0:T(8,128)(2,1)} async-done(((bf16[128,32,256]{2,1,0:T(8,128)(2,1)}), bf16[128,32,256]{2,1,0:T(8,128)(2,1)}, u32[]{:S(2)}, u32[]{:S(2)}) %all-to-all-start) | async-done | bytes 2097184 | tf_op jit(solution)/shard_map/all_to_all | solution.py:84
  236.6 11.9 %reshape.27 = bf16[8,16,32,2,4,32]{5,4,3,2,1,0:T(4,128)(2,1)} reshape(bf16[128,32,256]{2,1,0:T(8,128)(2,1)} %all-to-all-done) | data formatting | bytes 4194304 | tf_op jit(solution)/shard_map/reshape | solution.py:85
  248.5 12.0 %copy.58 = bf16[16,32,2,4,8,32]{5,4,1,0,3,2:T(8,128)(2,1)} copy(bf16[16,32,2,4,8,32]{5,3,2,1,0,4:T(4,128)(2,1)} %bitcast.89) | data formatting | bytes 4194304 | tf_op jit(solution)/shard_map/transpose | solution.py:86
  260.5 10.7 %reshape.28 = bf16[512,2,4,256]{3,0,2,1:T(8,128)(2,1)} reshape(bf16[16,32,2,4,8,32]{5,4,1,0,3,2:T(8,128)(2,1)} %copy.58) | data formatting | bytes 4194304 | tf_op jit(solution)/shard_map/reshape | solution.py:86
  283.2 11.0 %copy.61 = f32[512,1,2048]{2,1,0:T(1,128)} copy(f32[512,1,2048]{0,2,1:T(8,128)} %bitcast.95) | data formatting | bytes 8388608 | tf_op jit(solution)/shard_map/stack | solution.py:47
  294.2 7.5 %add_subtract_fusion = f32[4,512,512]{1,2,0:T(8,128)} fusion(f32[4,512,512]{1,2,0:T(8,128)} %fusion.11, f32[4,512,512]{1,2,0:T(8,128)} %fusion.9, f32[4,512,512]{1,2,0:T(8,128)} %fusion.19, bf16[256,4,512]{0,2,1:T(8,128)(2,1)S(1)} %bitcast.82, bf16[512,4,256]{0,2,1:T(8,128)(2,1)S(1)} %fusion.7), kind=kOutput, calls=%fused_computation.10 | convolution fusion | flops 540016640 | bytes 18874368 | tf_op jit(solution)/shard_map/rbk,kbf->rbf/dot_general | solution.py:21
  301.7 11.0 %copy.62 = f32[512,1,2048]{2,1,0:T(1,128)} copy(f32[512,1,2048]{0,2,1:T(8,128)} %bitcast.94) | data formatting | bytes 8388608 | tf_op jit(solution)/shard_map/stack | solution.py:47
  312.7 10.0 %pad_maximum_fusion = f32[512,2,2048]{2,1,0:T(2,128)} fusion(f32[512,1,2048]{2,1,0:T(1,128)} %copy.62, f32[512,1,2048]{2,1,0:T(1,128)} %copy.61), kind=kLoop, calls=%fused_computation.9 | loop fusion | flops 2097152 | bytes 16777216 | tf_op jit(solution)/shard_map/stack | solution.py:47
  324.6 158.0 %all-reduce.3.cloned.1.call-done = f32[512,2,2048]{2,1,0:T(2,128)} async-done(((f32[512,2,2048]{2,1,0:T(2,128)}), f32[512,2,2048]{2,1,0:T(2,128)}) %all-reduce.3.cloned.1.call-update) | async-done | bytes 8388624
  (63 shorter events, 59.0 us)
Async XLA Ops:
  6.5 57.6 %all-gather.3.cloned.1.call-start = ((), (), s32[]{:S(2)}) async-start(), calls=%async_computation.1 | async-start | bytes 2359296 | tf_op jit(solution)/shard_map/all_gather | solution.py:60
  7.3 114.7 %all-gather.5.cloned.1.call-start = ((), (), s32[]{:S(2)}) async-start(), calls=%async_computation.2 | async-start | bytes 4456448 | tf_op jit(solution)/shard_map/all_gather | solution.py:59
  153.1 2.5 copy-start.1
  153.1 4.7 copy-start.8
  158.6 3.8 copy-start.5
  162.4 7.6 %copy-start = (bf16[512,1,2048]{0,2,1:T(8,128)(2,1)S(1)}, bf16[512,1,2048]{0,2,1:T(8,128)(2,1)}, u32[]{:S(2)}) copy-start(bf16[512,1,2048]{0,2,1:T(8,128)(2,1)} %copy.77) | copy-start | bytes 6291460
  162.4 7.6 %copy-start.7 = (f32[512,4,256]{0,2,1:T(8,128)S(1)}, f32[512,4,256]{0,2,1:T(8,128)}, u32[]{:S(2)}) copy-start(f32[512,4,256]{0,2,1:T(8,128)} %copy.81) | copy-start | bytes 6291460
  162.4 7.6 %copy-start.9 = (f32[4,256,512]{2,1,0:T(8,128)S(1)}, f32[4,256,512]{2,1,0:T(8,128)}, u32[]{:S(2)}) copy-start(f32[4,256,512]{2,1,0:T(8,128)} %fusion.17) | copy-start | bytes 6291460
  174.8 5.6 %copy-start.4 = (bf16[16,32,1,4,8,32]{1,3,2,5,0,4:T(4,128)(2,1)S(1)}, bf16[16,32,1,4,8,32]{1,3,2,5,0,4:T(4,128)(2,1)}, u32[]{:S(2)}) copy-start(bf16[16,32,1,4,8,32]{1,3,2,5,0,4:T(4,128)(2,1)} %copy.56) | copy-start | bytes 3145732
  201.2 35.4 %all-to-all-start = ((bf16[128,32,256]{2,1,0:T(8,128)(2,1)}), bf16[128,32,256]{2,1,0:T(8,128)(2,1)}, u32[]{:S(2)}, u32[]{:S(2)}) async-start(bf16[128,32,256]{2,1,0:T(8,128)(2,1)} %reshape.26), calls=%async_computation | async-start | bytes 4194304 | tf_op jit(solution)/shard_map/all_to_all | solution.py:84
  207.3 275.3 %all-reduce.3.cloned.1.call-start = ((), (), s32[]{:S(2)}) async-start(), calls=%async_computation.3 | async-start | bytes 16777216
  207.3 4.0 copy-start.6
  271.3 2.1 copy-start.2
  276.8 3.4 copy-start.3
  322.7 0.7 copy-start.10
Sparse Core Ops, SparseCore 0:
  9.0 55.0 all-gather.2
  66.6 55.3 all-gather.4
  322.9 159.6 all-reduce.2
where the time goes:
time: 494 us; the launch traced here: 491 us
  waiting for transfers between devices  254 us (51%)
  local copies, waits for them, and re-layouts  148 us (30%)
  matrix products  49.3 us (10%)
  other arithmetic  20.4 us (4%)
  between operations  13.9 us (3%)
  starting transfers between devices  6.15 us (1%)
    unnamed x4, waiting for transfers between devices  159 us
    all_gather x1, waiting for transfers between devices, per_device(): rows_panel = lax.all_gather(records, 'sub', axis=0, tiled=True)  45 us
    unnamed x30, local copies, waits for them, and re-layouts  35.2 us
    all_gather x1, waiting for transfers between devices, per_device(): cols_panel = lax.all_gather(records, 'grp', axis=0, tiled=True)  26.7 us
    dot_general x8, matrix products, toward_columns(): jnp.einsum('rbk,kbf->rbf', left, right, preferred_element_type=jnp.float32)  25.4 us
    all_to_all x1, waiting for transfers between devices, per_device(): lax.all_to_all(blocks, ('grp', 'sub'), split_axis=0, concat_axis=0, tiled...  22.6 us
    another operation x2, local copies, waits for them, and re-layouts, full_term(): jnp.stack((part_re, part_im), axis=1).reshape(count, 2, frequency_grid)  22 us
    another operation x4, local copies, waits for them, and re-layouts, per_device(): stacked = jnp.stack((residual_real_part, residual_imaginary), axis=1)  21 us
  transfers between devices with their start and end apart: 4, of which 4 were waited for; matrix products, arithmetic and copies ran while one was open for 10% of the time, Pallas kernels for 0%

commit v1 on v0

v1 whole, which is shorter than its diff:
```python
import math

import jax
import jax.numpy as jnp
from jax import lax
from jax.experimental import pallas as pl
from jax.experimental.pallas import tpu as pltpu
from jax.sharding import PartitionSpec as P

RING = 4
CORES = 2
BANDS = 4
STAGES = 2
STAT = 32
WIDTH = 1024
HALF = 512
COLS = 1024
ROWS = 256
BLOCK = 256
MESH = pl.DeviceIdType.MESH
OPP, PLUS, MINUS, OWN = 0, 1, 2, 3
ROW_SHIFT = (2, 1, 3, 0)


def wrap(value):
    return lax.rem(value + RING, RING)


def device(x, y, z, core):
    return (y * 2 + lax.rem(x, 2), lax.div(x, 2) * 8 + z * 2 + core)


def kernel(
    x_ref, bins_row, bins_col, table_ref, out_ref,
    ybuf, lbuf, d1buf, d2buf, dbuf, sbuf, pbuf, rs1, gbuf, fbuf,
    hop_send, q_send, half_send, bin_send, rs_send, fin_send,
    own_recv, p_recv, q_recv, x_recv, d_recv, rs_recv, f_recv,
):
    grp = lax.axis_index("grp")
    sub = lax.axis_index("sub")
    y, x_lo = lax.div(grp, 2), lax.rem(grp, 2)
    x_hi, z, c = lax.div(sub, 8), lax.rem(lax.div(sub, 2), RING), lax.rem(sub, 2)
    x = x_hi * 2 + x_lo
    other = 1 - c
    scale = 2.0 / math.sqrt(HALF)

    def place(yy, zz, k):
        return (yy * RING + zz) * CORES + k

    def flow(k, p, q):
        yy = wrap(y + (1 - k) * p + k * q)
        zz = wrap(z + k * p + (1 - k) * q)
        return yy, zz

    def slot(k, p, q):
        yy, zz = flow(k, p, q)
        return place(yy, zz, k)

    def start(src, dst, send, recv, target):
        pltpu.make_async_remote_copy(
            src_ref=src, dst_ref=dst, send_sem=send, recv_sem=recv,
            device_id=target, device_id_type=MESH,
        ).start()

    def await_bytes(ref, sem):
        pltpu.make_async_copy(ref, ref, sem).wait()

    barrier = pltpu.get_barrier_semaphore()
    chips = []
    for dx in (1, 2, 3):
        chips.append((wrap(x + dx), y, z))
    for dy in (1, 2, 3):
        chips.append((x, wrap(y + dy), z))
        chips.append((wrap(x + 2), wrap(y + dy), z))
    flip = x + 1 - 2 * x_lo
    for dz in (1, 2, 3):
        chips.append((x, y, wrap(z + dz)))
        chips.append((flip, y, wrap(z + dz)))
    pl.semaphore_signal(barrier, inc=1, device_id=device(x, y, z, other), device_id_type=MESH)
    for chip in chips:
        for core in range(CORES):
            pl.semaphore_signal(barrier, inc=1, device_id=device(*chip, core), device_id_type=MESH)
    pl.semaphore_wait(barrier, len(chips) * CORES + 1)

    def first_hop(t):
        here = slot(c, 0, 0)
        start(x_ref.at[2 * other + t], ybuf.at[t, here], hop_send.at[t], own_recv.at[t],
              device(x, y, z, other))
        for sign, index in ((1, 0), (-1, 1)):
            yy, zz = flow(c, sign, 0)
            for core in range(CORES):
                start(x_ref.at[2 * core + t], ybuf.at[t, here], hop_send.at[t],
                      p_recv.at[t, c, index], device(x, yy, zz, core))

    def first_rows(t):
        for sign, index, row in ((1, 0, MINUS), (-1, 1, PLUS)):
            for core in range(CORES):
                start(x_ref.at[2 * core + t], lbuf.at[t, 0, row, c], hop_send.at[t],
                      x_recv.at[t, c, index], device(wrap(x + sign), y, z, core))

    def q_out(t, k, p, p_index):
        here = slot(k, p, 0)
        for sign, index in ((1, 0), (-1, 1)):
            yy, zz = flow(k, 0, sign)
            start(ybuf.at[t, here], ybuf.at[t, here], q_send.at[t],
                  q_recv.at[t, k, p_index, index], device(x, yy, zz, c))

    def own_local(t):
        mine = x_ref[2 * c + t]
        ybuf[t, slot(c, 0, 0)] = mine
        lbuf[t, 0, OWN, c] = mine
        q_out(t, c, 0, 0)

    def own_remote(t):
        here = slot(other, 0, 0)
        await_bytes(ybuf.at[t, here], own_recv.at[t])
        q_out(t, other, 0, 0)
        lbuf[t, 0, OWN, other] = ybuf[t, here]

    def p_step(t):
        for sign, index in ((-1, 0), (1, 1)):
            for k in range(CORES):
                here = slot(k, sign, 0)
                await_bytes(ybuf.at[t, here], p_recv.at[t, k, index])
                q_out(t, k, sign, 1 + index)
                yy, zz = flow(k, -sign, 0)
                part = pl.ds(16 * index, 16)
                start(ybuf.at[t, here, part], ybuf.at[t, here, part], half_send.at[t],
                      p_recv.at[t, k, 2], device(x, yy, zz, c))

    def p_last(t):
        for k in range(CORES):
            await_bytes(ybuf.at[t, slot(k, 2, 0)], p_recv.at[t, k, 2])
            q_out(t, k, 2, 3)

    def x_step(t):
        for row, index, sign in ((MINUS, 0, 1), (PLUS, 1, -1)):
            for k in range(CORES):
                await_bytes(lbuf.at[t, 0, row, k], x_recv.at[t, k, index])
                part = pl.ds(16 * index, 16)
                start(lbuf.at[t, 0, row, k, part], lbuf.at[t, 0, OPP, k, part], half_send.at[t],
                      x_recv.at[t, k, 2], device(wrap(x + sign), y, z, c))

    def x_last(t):
        for k in range(CORES):
            await_bytes(lbuf.at[t, 0, OPP, k], x_recv.at[t, k, 2])
        for row in range(RING):
            for k in range(CORES):
                lbuf[t, 1, row, k, :, :HALF] = lbuf[t, 0, row, k, :, HALF:]
                lbuf[t, 1, row, k, :, HALF:] = -lbuf[t, 0, row, k, :, :HALF]

    SHIFT = (0, -1, 1, 2)

    def q_step(t, p_index):
        p = SHIFT[p_index]
        for sign, index in ((-1, 0), (1, 1)):
            for k in range(CORES):
                here = slot(k, p, sign)
                await_bytes(ybuf.at[t, here], q_recv.at[t, k, p_index, index])
                yy, zz = flow(k, 0, -sign)
                part = pl.ds(16 * index, 16)
                start(ybuf.at[t, here, part], ybuf.at[t, here, part], half_send.at[t],
                      q_recv.at[t, k, p_index, 2], device(x, yy, zz, c))

    def q_last(t, k, p_index):
        await_bytes(ybuf.at[t, slot(k, SHIFT[p_index], 2)], q_recv.at[t, k, p_index, 2])

    def send_bins():
        here = z * CORES + c
        for turn in range(2):
            for dz in range(RING):
                to_x = x if turn == 0 else flip
                to_lo = lax.rem(to_x, 2)
                to_z = wrap(z + dz)
                for core in range(CORES):
                    src = bins_row.at[to_lo, :, to_z]
                    dst = d1buf.at[here, :, x_lo]
                    if turn == 0 and dz == 0:
                        @pl.when(core == c)
                        def _():
                            pltpu.make_async_copy(src, dst, d_recv.at[0]).start()

                        @pl.when(core != c)
                        def _():
                            start(src, dst, bin_send.at[0], d_recv.at[0], device(to_x, y, to_z, core))
                    else:
                        start(src, dst, bin_send.at[0], d_recv.at[0], device(to_x, y, to_z, core))
        for turn in range(2):
            for dy in range(RING):
                to_hi = x_hi if turn == 0 else 1 - x_hi
                to_x = to_hi * 2 + x_lo
                to_y = wrap(y + dy)
                for core in range(CORES):
                    src = bins_col.at[to_hi, to_y]
                    dst = d2buf.at[y, x_hi, :, c]
                    if turn == 0 and dy == 0:
                        @pl.when(core == c)
                        def _():
                            pltpu.make_async_copy(src, dst, d_recv.at[1]).start()

                        @pl.when(core != c)
                        def _():
                            start(src, dst, bin_send.at[1], d_recv.at[1], device(to_x, to_y, z, core))
                    else:
                        start(src, dst, bin_send.at[1], d_recv.at[1], device(to_x, to_y, z, core))

    def wait_bins():
        await_bytes(d1buf, d_recv.at[0])
        await_bytes(d2buf, d_recv.at[1])

    def lookups():
        names = []
        for t in range(STAGES):
            for part in range(2):
                line = table_ref[pl.ds(BANDS * part + 2 * c + t, 1), :]
                names.append(jnp.broadcast_to(line, (64, 128)))

        def one_row(row, carry):
            rx = lax.rem(x + jnp.where(row == 0, 2, jnp.where(row == 1, 1, jnp.where(row == 2, 3, 0))), RING)
            rhi, rlo = lax.div(rx, 2), lax.rem(rx, 2)
            pieces = [d1buf[zk, rhi, rlo].astype(jnp.float32) for zk in range(8)]
            for yy in range(RING):
                mirrored = d2buf[yy, rhi, rlo].astype(jnp.float32).astype(jnp.int32).reshape(64, BLOCK)
                for side in range(2):
                    direct = jnp.concatenate(
                        [pieces[4 * side + i][:, yy * STAT:(yy + 1) * STAT] for i in range(4)], axis=1
                    ).astype(jnp.int32)
                    mirror = mirrored[:, side * 128:(side + 1) * 128]
                    for t in range(STAGES):
                        for part in range(2):
                            tab = names[2 * t + part]
                            one = jnp.take_along_axis(tab, direct, axis=1)
                            two = jnp.take_along_axis(tab, mirror, axis=1)
                            value = one + two if part == 0 else one - two
                            dbuf[t, part, row, :, pl.ds(yy * BLOCK + side * 128, 128)] = value
            return carry

        lax.fori_loop(0, RING, one_row, 0)

    def corr(t, dy):
        yy = wrap(y + dy)
        base = pl.multiple_of(yy * BLOCK, BLOCK)
        right = ybuf[t, pl.ds(yy * 8, 8)].reshape(BLOCK, WIDTH)
        for part in range(2):
            left = lbuf[t, part].reshape(ROWS, WIDTH)
            got = lax.dot_general(left, right, (((1,), (1,)), ((), ())),
                                  preferred_element_type=jnp.float32)
            value = got.reshape(RING, 64, BLOCK) * scale - dbuf[t, part, :, :, pl.ds(base, BLOCK)]
            sbuf[t, :, part, :, pl.ds(base, BLOCK)] = value.astype(jnp.bfloat16)

    def adjoint(t, half):
        left = sbuf[t, 2 * half:2 * half + 2].reshape(ROWS, COLS)
        for j in range(2):
            real = ybuf[t, :, :, j * 256:(j + 1) * 256].reshape(COLS, 256)
            imag = ybuf[t, :, :, HALF + j * 256:HALF + (j + 1) * 256].reshape(COLS, 256)
            a = jnp.dot(left, real, preferred_element_type=jnp.float32).reshape(2, 2, 64, 256)
            b = jnp.dot(left, imag, preferred_element_type=jnp.float32).reshape(2, 2, 64, 256)
            re = (a[:, 0] - b[:, 1]).reshape(2, CORES, STAT, 256)
            im = (b[:, 0] + a[:, 1]).reshape(2, CORES, STAT, 256)
            pbuf[t, 2 * half:2 * half + 2, :, :, j * 256:(j + 1) * 256] = re
            pbuf[t, 2 * half:2 * half + 2, :, :, HALF + j * 256:HALF + (j + 1) * 256] = im

    def sums_first(t):
        up, down = wrap(x + 1), wrap(x - 1)
        start(pbuf.at[t, OPP, 0], rs1.at[t, 0], rs_send.at[t], rs_recv.at[t, 0], device(up, y, z, c))
        start(pbuf.at[t, OPP, 1], rs1.at[t, 1], rs_send.at[t], rs_recv.at[t, 1], device(down, y, z, c))
        start(pbuf.at[t, PLUS, 1], fbuf.at[c, t, 0], rs_send.at[t], f_recv.at[c, t, 0], device(up, y, z, 1))

    def sums_second(t):
        down = wrap(x - 1)
        start(pbuf.at[t, MINUS, 0], fbuf.at[c, t, 1], rs_send.at[t], f_recv.at[c, t, 1], device(down, y, z, 0))
        start(pbuf.at[t, OWN, other], fbuf.at[c, t, 2], rs_send.at[t], f_recv.at[c, t, 2],
              device(x, y, z, other))

    def sums_forward(t):
        await_bytes(rs1.at[t, 0], rs_recv.at[t, 0])
        gbuf[t, 0] = rs1[t, 0] + pbuf[t, PLUS, 0]
        start(gbuf.at[t, 0], fbuf.at[c, t, 0], fin_send.at[t], f_recv.at[c, t, 0],
              device(wrap(x + 1), y, z, 0))
        await_bytes(rs1.at[t, 1], rs_recv.at[t, 1])
        gbuf[t, 1] = rs1[t, 1] + pbuf[t, MINUS, 1]
        start(gbuf.at[t, 1], fbuf.at[c, t, 1], fin_send.at[t], f_recv.at[c, t, 1],
              device(wrap(x - 1), y, z, 1))

    def sums_last(t):
        total = 1.0 / math.sqrt(COLS * RING)
        for i in range(2):
            await_bytes(fbuf.at[c, t, i], f_recv.at[c, t, i])
        out_ref[2 * c + t] = (fbuf[c, t, 0] + fbuf[c, t, 1] + pbuf[t, OWN, c]) * total
        for i in range(3):
            await_bytes(fbuf.at[other, t, i], f_recv.at[other, t, i])
        out_ref[2 * other + t] = (fbuf[other, t, 0] + fbuf[other, t, 1] + fbuf[other, t, 2]) * total

    def sends_done(t):
        await_bytes(ybuf.at[t, pl.ds(0, 9)], hop_send.at[t])
        await_bytes(ybuf.at[t, pl.ds(0, 16)], q_send.at[t])
        await_bytes(ybuf.at[t, pl.ds(0, 12)], half_send.at[t])

    first_hop(0)
    own_local(0)
    own_remote(0)
    first_rows(0)
    send_bins()
    p_step(0)
    x_step(0)
    p_last(0)
    first_hop(1)
    first_rows(1)
    q_step(0, 0)
    own_local(1)
    own_remote(1)
    p_step(1)
    x_step(1)
    wait_bins()
    lookups()
    x_last(0)
    q_step(0, 1)
    q_step(0, 2)
    p_last(1)
    q_last(0, 0, 0)
    corr(0, 0)
    q_step(0, 3)
    x_last(1)
    q_last(0, 0, 2)
    corr(0, 1)
    q_last(0, 0, 1)
    corr(0, -1)
    q_step(1, 0)
    q_last(0, 0, 3)
    for i in range(4):
        q_last(0, 1, i)
    corr(0, 2)
    adjoint(0, 0)
    sums_first(0)
    q_step(1, 1)
    q_step(1, 2)
    adjoint(0, 1)
    sums_second(0)
    q_last(1, 0, 0)
    corr(1, 0)
    sums_forward(0)
    q_step(1, 3)
    q_last(1, 0, 2)
    corr(1, 1)
    q_last(1, 0, 1)
    corr(1, -1)
    sends_done(0)
    for i in range(2):
        await_bytes(ybuf.at[0, pl.ds(0, 15), pl.ds(0, 16)], bin_send.at[i])
    q_last(1, 0, 3)
    for i in range(4):
        q_last(1, 1, i)
    corr(1, 2)
    adjoint(1, 0)
    sums_first(1)
    adjoint(1, 1)
    sums_second(1)
    sums_forward(1)
    sums_last(0)
    sends_done(1)
    sums_last(1)
    for t in range(STAGES):
        await_bytes(ybuf.at[t, pl.ds(0, 10)], rs_send.at[t])
        await_bytes(gbuf.at[t], fin_send.at[t])


def exchange(spectra, bins_row, bins_col, table):
    f32, bf16 = jnp.float32, jnp.bfloat16
    dma = pltpu.SemaphoreType.DMA
    vmem = pl.BlockSpec(memory_space=pltpu.VMEM)
    return pl.pallas_call(
        kernel,
        out_shape=jax.ShapeDtypeStruct((BANDS, STAT, WIDTH), f32),
        in_specs=[vmem] * 4,
        out_specs=vmem,
        scratch_shapes=[
            pltpu.VMEM((STAGES, 32, STAT, WIDTH), bf16),
            pltpu.VMEM((STAGES, 2, RING, CORES, STAT, WIDTH), bf16),
            pltpu.VMEM((8, 2, 2, 64, 128), bf16),
            pltpu.VMEM((RING, 2, 2, CORES, STAT, BLOCK), bf16),
            pltpu.VMEM((STAGES, 2, RING, 64, COLS), f32),
            pltpu.VMEM((STAGES, RING, 2, 64, COLS), bf16),
            pltpu.VMEM((STAGES, RING, CORES, STAT, WIDTH), f32),
            pltpu.VMEM((STAGES, 2, STAT, WIDTH), f32),
            pltpu.VMEM((STAGES, 2, STAT, WIDTH), f32),
            pltpu.VMEM((CORES, STAGES, 3, STAT, WIDTH), f32),
            dma((STAGES,)), dma((STAGES,)), dma((STAGES,)), dma((2,)), dma((STAGES,)), dma((STAGES,)),
            dma((STAGES,)), dma((STAGES, CORES, 3)), dma((STAGES, CORES, 4, 3)),
            dma((STAGES, CORES, 3)), dma((2,)), dma((STAGES, 2)), dma((CORES, STAGES, 3)),
        ],
        compiler_params=pltpu.CompilerParams(
            collective_id=0, has_side_effects=True, vmem_limit_bytes=48 * 1024 * 1024
        ),
    )(spectra, bins_row, bins_col, table)


def per_device(records, ref_bin, ref_table):
    spectra = records.reshape(STAT, 2, BANDS, HALF).transpose(2, 0, 1, 3).reshape(BANDS, STAT, WIDTH)
    tile = ref_bin[0, :, 0, :].astype(jnp.bfloat16)
    bins_row = tile.reshape(2, RING, 64, RING, 2, STAT).transpose(4, 0, 1, 2, 3, 5)
    bins_row = bins_row.reshape(2, 2, RING, 64, 128)
    bins_col = tile.reshape(2, BLOCK, RING, 2, STAT).transpose(0, 2, 3, 4, 1)
    table = jnp.pad(ref_table.astype(jnp.float32).T, ((0, 0), (0, 64)))
    out = exchange(spectra, bins_row, bins_col, table)
    return out.reshape(BANDS, STAT, 2, HALF).transpose(1, 2, 0, 3).reshape(STAT, 2, BANDS * HALF)


def solution(mesh):
    in_specs = (P(("grp", "sub"), None, None), P("grp", None, "sub", None), P())
    out_specs = P(("grp", "sub"), None, None)
    return jax.shard_map(
        per_device, mesh=mesh, in_specs=in_specs, out_specs=out_specs, check_vma=False
    )
```

time: 494 us -> 71.8 us (0.15)
  waiting for transfers between devices: 254 us -> 0 us
  local copies, waits for them, and re-layouts: 148 us -> 4.42 us
  Pallas kernels: 0 us -> 65.5 us
  matrix products: 49.3 us -> 0 us
  other arithmetic: 20.4 us -> 1.41 us
  between operations: 13.9 us -> 0.09 us
  starting transfers between devices: 6.15 us -> 0 us
    unnamed x4 -> x0, waiting for transfers between devices: 159 us -> none
    all_gather x2 -> x0, waiting for transfers between devices: 71.7 us -> none  [the longest x1 45 us: per_device(): rows_panel = lax.all_gather(records, 'sub', axis=0, tiled=True)]
    pallas_call x0 -> x1, Pallas kernels: none -> 65.5 us  [exchange(): pl.pallas_call(kernel, out_shape=jax.ShapeDtypeStruct((BANDS, STAT, WIDTH...]
    dot_general x20 -> x0, matrix products: 49.3 us -> none  [the longest x8 25.4 us: toward_columns(): jnp.einsum('rbk,kbf->rbf', left, right, preferred_element_type=jnp.float32)]
    another operation x6 -> x0, local copies, waits for them, and re-layouts: 43 us -> none  [the longest x2 22 us: full_term(): jnp.stack((part_re, part_im), axis=1).reshape(count, 2, frequency_grid)]
    unnamed x30 -> x4, local copies, waits for them, and re-layouts: 35.2 us -> 1.41 us
    reshape x3 -> x5, local copies, waits for them, and re-layouts: 35.1 us -> 1.87 us  [the longest x2 1.3 us: per_device(): out.reshape(BANDS, STAT, 2, HALF).transpose(1, 2, 0, 3)]
    all_to_all x1 -> x0, waiting for transfers between devices: 22.6 us -> none  [per_device(): lax.all_to_all(blocks, ('grp', 'sub'), split_axis=0, concat_axis=0, tiled...]
  transfers between devices with their start and end apart: 4 -> 0, of which waited for: 4 -> 0; matrix products, arithmetic and copies ran while one was open for 10% -> 0% of each run, Pallas kernels for 0% -> 0%
where the time goes in v1:
time: 71.8 us; the launch traced here: 71.4 us
  Pallas kernels  65.5 us (91%)
  local copies, waits for them, and re-layouts  4.42 us (6%)
  other arithmetic  1.41 us (2%)
    pallas_call x1, Pallas kernels, exchange(): pl.pallas_call(kernel, out_shape=jax.ShapeDtypeStruct((BANDS, STAT, WIDTH...  65.5 us

profile of v1, /device:TPU:1, one launch (start us, length us, event | category | flops | bytes accessed | tf_op | source)
XLA Modules:
  0.0 71.4 jit_solution(16394693751678281842)
XLA Ops:
  0.0 1.4 %convert_element_type.14 = bf16[1,512,1,256]{3,2,1,0:T(2,128)(2,1)S(1)} convert(s32[1,512,1,256]{3,2,1,0:T(1,128)} %param.4) | non-fusion elementwise | flops 131072 | bytes 786432 | tf_op jit(solution)/shard_map/convert_element_type | solution.py:399
  1.4 0.7 copy.8
  2.1 0.3 convert_element_type.15
  2.4 0.1 copy.9
  2.5 0.2 copy.12.bins_row
  2.7 0.1 convert_element_type.16
  2.8 0.0 copy-start
  2.8 0.9 %copy-done = bf16[32,2,2048]{2,1,0:T(2,128)(2,1)S(1)} copy-done((bf16[32,2,2048]{2,1,0:T(2,128)(2,1)S(1)}, bf16[32,2,2048]{2,1,0:T(2,128)(2,1)}, u32[]{:S(2)}) %copy-start) | copy-done | bytes 262168
  3.7 0.2 copy.18
  3.9 0.0 copy-start.1
  3.9 0.2 reshape.22.x_ref
  4.1 0.5 copy-done.1
  4.6 65.5 %shard_map.37 = f32[4,32,1024]{2,1,0:T(8,128)S(1)} custom-call(bf16[4,32,1024]{2,1,0:T(8,128)(2,1)S(1)} %reshape.22.x_ref, bf16[2,2,4,64,128]{4,3,2,1,0:T(8,128)(2,1)S(1)} %copy.12.bins_row, bf16[2,4,2,32,256]{4,3,2,1,0:T(8,128)(2,1)S(1)} %bitcast.24, f32[8,128]{1,0:T(8,128)S(1)} %pad_convert_fusion.table_ref), custom_call_target="tpu_custom_call" | custom-call | tf_op jit(solution)/shard_map/pallas_call | solution.py:371
  70.1 0.4 reshape.24
  70.6 0.9 %copy.15 = f32[4,32,1,2,512]{4,3,0,2,1:T(2,128)} copy(f32[4,32,1,2,512]{4,3,2,1,0:T(2,128)S(1)} %bitcast.26) | data formatting | bytes 1048576 | tf_op jit(solution)/shard_map/reshape | solution.py:405
  (2 shorter events, 0.0 us)
Async XLA Ops:
  2.8 1.0 %copy-start = (bf16[32,2,2048]{2,1,0:T(2,128)(2,1)S(1)}, bf16[32,2,2048]{2,1,0:T(2,128)(2,1)}, u32[]{:S(2)}) copy-start(bf16[32,2,2048]{2,1,0:T(2,128)(2,1)} %param.3) | copy-start | bytes 786436
  3.9 0.7 copy-start.1

commit v2 on v1

v2 whole, which is shorter than its diff:
```python
import math

import jax
import jax.numpy as jnp
from jax import lax
from jax.experimental import pallas as pl
from jax.experimental.pallas import tpu as pltpu
from jax.sharding import PartitionSpec as P

RING = 4
CORES = 2
BANDS = 4
STAGES = 2
STAT = 32
WIDTH = 1024
HALF = 512
COLS = 1024
ROWS = 256
BLOCK = 256
MESH = pl.DeviceIdType.MESH
OPP, PLUS, MINUS, OWN = 0, 1, 2, 3
ROW_SHIFT = (2, 1, 3, 0)


def wrap(value):
    return lax.rem(value + RING, RING)


def device(x, y, z, core):
    return (y * 2 + lax.rem(x, 2), lax.div(x, 2) * 8 + z * 2 + core)


def kernel(
    raw_x, raw_bins, raw_table, out_ref,
    xraw, xwide, xbuf, braw, table, brow, bcol,
    ybuf, lbuf, d1buf, d2buf, dbuf, sbuf, pbuf, hbuf, rs1, gbuf, fbuf, nbuf,
    in_sem, hop_send, q_send, half_send, bin_send, rs_send, fin_send, own_send,
    own_recv, p_recv, q_recv, x_recv, d_recv, rs_recv, f_recv, n_recv,
):
    grp = lax.axis_index("grp")
    sub = lax.axis_index("sub")
    y, x_lo = lax.div(grp, 2), lax.rem(grp, 2)
    x_hi, z, c = lax.div(sub, 8), lax.rem(lax.div(sub, 2), RING), lax.rem(sub, 2)
    x = x_hi * 2 + x_lo
    other = 1 - c
    flip = x + 1 - 2 * x_lo
    scale = 2.0 / math.sqrt(HALF)
    f32, bf16 = jnp.float32, jnp.bfloat16

    def flow(k, p, q):
        yy = wrap(y + (1 - k) * p + k * q)
        zz = wrap(z + k * p + (1 - k) * q)
        return yy, zz

    def slot(k, p, q):
        yy, zz = flow(k, p, q)
        return (yy * RING + zz) * CORES + k

    def start(src, dst, send, recv, target):
        pltpu.make_async_remote_copy(
            src_ref=src, dst_ref=dst, send_sem=send, recv_sem=recv,
            device_id=target, device_id_type=MESH,
        ).start()

    def await_bytes(ref, sem):
        pltpu.make_async_copy(ref, ref, sem).wait()

    loads = [
        pltpu.make_async_copy(raw_x, xraw, in_sem.at[0]),
        pltpu.make_async_copy(raw_bins, braw, in_sem.at[1]),
        pltpu.make_async_copy(raw_table, table.at[0], in_sem.at[2]),
    ]
    for load in loads:
        load.start()
    barrier = pltpu.get_barrier_semaphore()
    near = [(wrap(x + d), y, z) for d in (1, 3)]
    near += [(x, wrap(y + d), z) for d in (1, 3)]
    near += [(x, y, wrap(z + d)) for d in (1, 3)]
    far = [(wrap(x + 2), wrap(y + d), z) for d in range(RING)] + [(x, wrap(y + 2), z)]
    far += [(flip, y, wrap(z + d)) for d in (1, 2, 3)] + [(x, y, wrap(z + 2))]
    peers = [device(x, y, z, other)] + [device(*chip, c) for chip in near + far]
    peers += [device(*chip, other) for chip in near]
    for peer in peers:
        pl.semaphore_signal(barrier, inc=1, device_id=peer, device_id_type=MESH)

    loads[0].wait()
    xwide[...] = xraw[...].astype(f32)
    for band in range(BANDS):
        for part in range(2):
            for j in range(4):
                line = xwide[pl.ds((band * 4 + j) * 2 + part, STAT, stride=32), :]
                xbuf[band, :, part * HALF + j * 128:part * HALF + (j + 1) * 128] = line.astype(bf16)
    pl.semaphore_wait(barrier, len(peers))

    def first_hop(t):
        here = slot(c, 0, 0)
        for index, sign in ((0, 1), (1, -1)):
            yy, zz = flow(c, sign, 0)
            for core in range(CORES):
                start(xbuf.at[2 * core + t], ybuf.at[t, here], hop_send.at[t],
                      p_recv.at[t, c, index], device(x, yy, zz, core))
        for index, sign in ((0, 1), (1, -1)):
            yy, zz = flow(c, 0, sign)
            for core in range(CORES):
                start(xbuf.at[2 * core + t], ybuf.at[t, here], hop_send.at[t],
                      q_recv.at[t, c, 0, index], device(x, yy, zz, core))
        start(xbuf.at[2 * other + t], ybuf.at[t, here], hop_send.at[t], own_recv.at[t],
              device(x, y, z, other))
        for sign, index, row in ((1, 0, MINUS), (-1, 1, PLUS)):
            for core in range(CORES):
                start(xbuf.at[2 * core + t], lbuf.at[t, 0, row, c], hop_send.at[t],
                      x_recv.at[t, c, index], device(wrap(x + sign), y, z, core))

    def own_units(t):
        mine = xbuf[2 * c + t]
        ybuf[t, slot(c, 0, 0)] = mine
        lbuf[t, 0, OWN, c] = mine
        here = slot(other, 0, 0)
        await_bytes(ybuf.at[t, here], own_recv.at[t])
        lbuf[t, 0, OWN, other] = ybuf[t, here]

    SHIFT = (0, -1, 1, 2)

    def q_out(t, k, p_index):
        here = slot(k, SHIFT[p_index], 0)
        for sign, index in ((1, 0), (-1, 1)):
            yy, zz = flow(k, 0, sign)
            start(ybuf.at[t, here], ybuf.at[t, here], q_send.at[t],
                  q_recv.at[t, k, p_index, index], device(x, yy, zz, c))

    def p_step(t):
        for sign, index in ((-1, 0), (1, 1)):
            for k in range(CORES):
                here = slot(k, sign, 0)
                await_bytes(ybuf.at[t, here], p_recv.at[t, k, index])
                yy, zz = flow(k, -sign, 0)
                part = pl.ds(16 * index, 16)
                start(ybuf.at[t, here, part], ybuf.at[t, here, part], half_send.at[t],
                      p_recv.at[t, k, 2], device(x, yy, zz, c))

    def q_near(t):
        for p_index in (1, 2):
            for k in range(CORES):
                q_out(t, k, p_index)

    def p_last(t):
        for k in range(CORES):
            await_bytes(ybuf.at[t, slot(k, 2, 0)], p_recv.at[t, k, 2])
            q_out(t, k, 3)

    def x_step(t):
        for row, index, sign in ((MINUS, 0, 1), (PLUS, 1, -1)):
            for k in range(CORES):
                await_bytes(lbuf.at[t, 0, row, k], x_recv.at[t, k, index])
                part = pl.ds(16 * index, 16)
                start(lbuf.at[t, 0, row, k, part], lbuf.at[t, 0, OPP, k, part], half_send.at[t],
                      x_recv.at[t, k, 2], device(wrap(x + sign), y, z, c))

    def x_last(t):
        for k in range(CORES):
            await_bytes(lbuf.at[t, 0, OPP, k], x_recv.at[t, k, 2])
        for row in range(RING):
            for k in range(CORES):
                lbuf[t, 1, row, k, :, :HALF] = lbuf[t, 0, row, k, :, HALF:]
                lbuf[t, 1, row, k, :, HALF:] = -lbuf[t, 0, row, k, :, :HALF]

    def q_step(t, p_index):
        p = SHIFT[p_index]
        for sign, index in ((-1, 0), (1, 1)):
            for k in range(CORES):
                here = slot(k, p, sign)
                await_bytes(ybuf.at[t, here], q_recv.at[t, k, p_index, index])
                yy, zz = flow(k, 0, -sign)
                part = pl.ds(16 * index, 16)
                start(ybuf.at[t, here, part], ybuf.at[t, here, part], half_send.at[t],
                      q_recv.at[t, k, p_index, 2], device(x, yy, zz, c))

    def q_last(t, k, p_index):
        await_bytes(ybuf.at[t, slot(k, SHIFT[p_index], 2)], q_recv.at[t, k, p_index, 2])

    def make_bins():
        loads[1].wait()
        tile = jnp.concatenate(
            [braw[pl.ds(h, 512, stride=2), :].astype(f32).astype(bf16) for h in range(2)], axis=1
        )
        source = lax.broadcasted_iota(jnp.int32, (BLOCK, BLOCK), 0)
        column = lax.broadcasted_iota(jnp.int32, (BLOCK, BLOCK), 1)
        wanted = ((column // 32) % 4) * 64 + (column // 128) * 32 + column % 32
        order = (source == wanted).astype(bf16)
        same = (source == column).astype(bf16)
        by_row = jnp.dot(tile, order, preferred_element_type=f32).astype(bf16)
        for lo in range(2):
            brow[lo] = by_row[:, lo * 128:(lo + 1) * 128].reshape(2, RING, 64, 128)
        by_col = lax.dot_general(same, tile, (((1,), (1,)), ((), ())),
                                 preferred_element_type=f32).astype(bf16)
        for hi in range(2):
            bcol[hi] = by_col[:, hi * BLOCK:(hi + 1) * BLOCK].reshape(RING, 2, STAT, BLOCK)

    def send_bins():
        for turn in range(2):
            to_x = x if turn == 0 else flip
            to_lo = lax.rem(to_x, 2)
            for dz in range(RING):
                to_z = wrap(z + dz)
                src, dst = brow.at[to_lo, :, to_z], d1buf.at[c, z, :, x_lo]
                if turn == 0 and dz == 0:
                    pltpu.make_async_copy(src, dst, d_recv.at[0]).start()
                else:
                    start(src, dst, bin_send.at[0], d_recv.at[0], device(to_x, y, to_z, c))
        for turn in range(2):
            to_hi = x_hi if turn == 0 else 1 - x_hi
            for dy in range(RING):
                to_y = wrap(y + dy)
                src, dst = bcol.at[to_hi, to_y], d2buf.at[c, y, x_hi]
                if turn == 0 and dy == 0:
                    pltpu.make_async_copy(src, dst, d_recv.at[1]).start()
                else:
                    start(src, dst, bin_send.at[1], d_recv.at[1], device(to_hi * 2 + x_lo, to_y, z, c))

    def share_bins():
        await_bytes(d1buf.at[c], d_recv.at[0])
        start(d1buf.at[c], d1buf.at[c], bin_send.at[2], d_recv.at[2], device(x, y, z, other))
        await_bytes(d2buf.at[c], d_recv.at[1])
        start(d2buf.at[c], d2buf.at[c], bin_send.at[2], d_recv.at[3], device(x, y, z, other))

    def wait_bins():
        await_bytes(d1buf.at[other], d_recv.at[2])
        await_bytes(d2buf.at[other], d_recv.at[3])
        loads[2].wait()
        table[1] = table[0]

    def lookups(row):
        wide = jnp.concatenate([table[0], table[1]], axis=1).astype(f32)
        table_wide = wide
        names = []
        for t in range(STAGES):
            for part in range(2):
                line = table_line(table_wide, BANDS * part, t)
                names.append(jnp.broadcast_to(line, (64, 128)))
        rx = wrap(x + ROW_SHIFT[row])
        rhi, rlo = lax.div(rx, 2), lax.rem(rx, 2)
        pieces = [d1buf[k, zz, rhi, rlo].astype(f32) for zz in range(RING) for k in range(CORES)]
        for yy in range(RING):
            mirrored = d2buf[:, yy, rhi, rlo].astype(f32).astype(jnp.int32).reshape(64, BLOCK)
            for side in range(2):
                direct = jnp.concatenate(
                    [pieces[4 * side + i][:, yy * STAT:(yy + 1) * STAT] for i in range(4)], axis=1
                ).astype(jnp.int32)
                mirror = mirrored[:, side * 128:(side + 1) * 128]
                for t in range(STAGES):
                    for part in range(2):
                        tab = names[2 * t + part]
                        one = jnp.take_along_axis(tab, direct, axis=1)
                        two = jnp.take_along_axis(tab, mirror, axis=1)
                        value = one + two if part == 0 else one - two
                        dbuf[t, part, row, :, pl.ds(yy * BLOCK + side * 128, 128)] = value

    def table_line(wide, base, t):
        return jnp.where(c == 0, wide[base + t:base + t + 1], wide[base + 2 + t:base + 3 + t])

    def corr(t, dy):
        yy = wrap(y + dy)
        base = pl.multiple_of(yy * BLOCK, BLOCK)
        right = ybuf[t, pl.ds(yy * 8, 8)].reshape(BLOCK, WIDTH)
        for part in range(2):
            left = lbuf[t, part].reshape(ROWS, WIDTH)
            got = lax.dot_general(left, right, (((1,), (1,)), ((), ())), preferred_element_type=f32)
            value = got.reshape(RING, 64, BLOCK) * scale - dbuf[t, part, :, :, pl.ds(base, BLOCK)]
            sbuf[t, :, part, :, pl.ds(base, BLOCK)] = value.astype(bf16)

    def adjoint(t, half):
        left = sbuf[t, 2 * half:2 * half + 2].reshape(ROWS, COLS)
        for j in range(2):
            real = ybuf[t, :, :, j * 256:(j + 1) * 256].reshape(COLS, 256)
            imag = ybuf[t, :, :, HALF + j * 256:HALF + (j + 1) * 256].reshape(COLS, 256)
            a = jnp.dot(left, real, preferred_element_type=f32).reshape(2, 2, 64, 256)
            b = jnp.dot(left, imag, preferred_element_type=f32).reshape(2, 2, 64, 256)
            re = (a[:, 0] - b[:, 1]).reshape(2, CORES, STAT, 256)
            im = (b[:, 0] + a[:, 1]).reshape(2, CORES, STAT, 256)
            for value, base in ((re, j * 256), (im, HALF + j * 256)):
                pbuf[t, 2 * half:2 * half + 2, :, :, base:base + 256] = value
                hbuf[t, 2 * half:2 * half + 2, :, :, base:base + 256] = value.astype(bf16)

    def sums_first(t):
        up, down = wrap(x + 1), wrap(x - 1)
        start(hbuf.at[t, OPP, 0], rs1.at[t, 0], rs_send.at[t], rs_recv.at[t, 0], device(up, y, z, c))
        start(hbuf.at[t, OPP, 1], rs1.at[t, 1], rs_send.at[t], rs_recv.at[t, 1], device(down, y, z, c))
        start(hbuf.at[t, PLUS, 1], fbuf.at[c, t, 0], rs_send.at[t], f_recv.at[c, t, 0], device(up, y, z, 1))

    def sums_second(t):
        down = wrap(x - 1)
        start(hbuf.at[t, MINUS, 0], fbuf.at[c, t, 1], rs_send.at[t], f_recv.at[c, t, 1], device(down, y, z, 0))
        start(pbuf.at[t, OWN, other], nbuf.at[t], own_send.at[t], n_recv.at[t], device(x, y, z, other))

    def sums_forward(t):
        await_bytes(rs1.at[t, 0], rs_recv.at[t, 0])
        gbuf[t, 0] = (rs1[t, 0].astype(f32) + pbuf[t, PLUS, 0]).astype(bf16)
        start(gbuf.at[t, 0], fbuf.at[c, t, 0], fin_send.at[t], f_recv.at[c, t, 0],
              device(wrap(x + 1), y, z, 0))
        await_bytes(rs1.at[t, 1], rs_recv.at[t, 1])
        gbuf[t, 1] = (rs1[t, 1].astype(f32) + pbuf[t, MINUS, 1]).astype(bf16)
        start(gbuf.at[t, 1], fbuf.at[c, t, 1], fin_send.at[t], f_recv.at[c, t, 1],
              device(wrap(x - 1), y, z, 1))

    def store(band, value):
        value = value * (1.0 / math.sqrt(COLS * RING))
        for part in range(2):
            for j in range(4):
                piece = value[:, part * HALF + j * 128:part * HALF + (j + 1) * 128]
                out_ref[pl.ds(band * 8 + j * 2 + part, STAT, stride=32), :] = piece

    def sums_last(t):
        await_bytes(nbuf.at[t], n_recv.at[t])
        for core, mine in ((other, nbuf.at[t]), (c, pbuf.at[t, OWN, c])):
            for i in range(2):
                await_bytes(fbuf.at[core, t, i], f_recv.at[core, t, i])
            store(2 * core + t, mine[...] + fbuf[core, t, 0].astype(f32) + fbuf[core, t, 1].astype(f32))

    def sends_done(t):
        await_bytes(ybuf.at[t, pl.ds(0, 13)], hop_send.at[t])
        await_bytes(ybuf.at[t, pl.ds(0, 12)], q_send.at[t])
        await_bytes(ybuf.at[t, pl.ds(0, 12)], half_send.at[t])

    first_hop(0)
    first_hop(1)
    make_bins()
    send_bins()
    p_step(0)
    q_near(0)
    x_step(0)
    own_units(0)
    q_step(0, 0)
    p_step(1)
    x_step(1)
    own_units(1)
    share_bins()
    p_last(0)
    x_last(0)
    wait_bins()
    lookups(0)
    q_step(0, 1)
    q_step(0, 2)
    q_near(1)
    lookups(1)
    q_step(1, 0)
    q_step(0, 3)
    p_last(1)
    lookups(2)
    lookups(3)
    q_last(0, 0, 0)
    corr(0, 0)
    x_last(1)
    q_last(0, 0, 2)
    corr(0, 1)
    q_step(1, 1)
    q_step(1, 2)
    q_last(0, 0, 1)
    corr(0, -1)
    q_last(0, 0, 3)
    for i in range(4):
        q_last(0, 1, i)
    corr(0, 2)
    q_step(1, 3)
    adjoint(0, 0)
    sums_first(0)
    adjoint(0, 1)
    sums_second(0)
    q_last(1, 0, 0)
    corr(1, 0)
    sends_done(0)
    for i in range(2):
        await_bytes(ybuf.at[0, pl.ds(0, 7), pl.ds(0, 16)], bin_send.at[i])
    await_bytes(ybuf.at[0, pl.ds(0, 8)], bin_send.at[2])
    q_last(1, 0, 2)
    corr(1, 1)
    q_last(1, 0, 1)
    corr(1, -1)
    sums_forward(0)
    q_last(1, 0, 3)
    for i in range(4):
        q_last(1, 1, i)
    corr(1, 2)
    adjoint(1, 0)
    sums_first(1)
    adjoint(1, 1)
    sums_second(1)
    sums_last(0)
    sums_forward(1)
    sends_done(1)
    await_bytes(hbuf.at[0, pl.ds(0, 2)], rs_send.at[0])
    await_bytes(nbuf.at[0], own_send.at[0])
    await_bytes(gbuf.at[0], fin_send.at[0])
    sums_last(1)
    await_bytes(hbuf.at[1, pl.ds(0, 2)], rs_send.at[1])
    await_bytes(nbuf.at[1], own_send.at[1])
    await_bytes(gbuf.at[1], fin_send.at[1])


def exchange(spectra, bins, table):
    f32, bf16, i32 = jnp.float32, jnp.bfloat16, jnp.int32
    dma, vmem = pltpu.SemaphoreType.DMA, pltpu.VMEM
    return pl.pallas_call(
        kernel,
        out_shape=jax.ShapeDtypeStruct((STAT * 32, 128), f32),
        in_specs=[pl.BlockSpec(memory_space=pltpu.HBM)] * 3,
        out_specs=pl.BlockSpec(memory_space=pltpu.VMEM),
        scratch_shapes=[
            vmem((STAT * 32, 128), bf16),
            vmem((STAT * 32, 128), f32),
            vmem((BANDS, STAT, WIDTH), bf16),
            vmem((1024, 128), i32),
            vmem((2, 2 * BANDS, 64), bf16),
            vmem((2, 2, RING, 64, 128), bf16),
            vmem((2, RING, 2, STAT, BLOCK), bf16),
            vmem((STAGES, 32, STAT, WIDTH), bf16),
            vmem((STAGES, 2, RING, CORES, STAT, WIDTH), bf16),
            vmem((CORES, RING, 2, 2, 64, 128), bf16),
            vmem((CORES, RING, 2, 2, STAT, BLOCK), bf16),
            vmem((STAGES, 2, RING, 64, COLS), f32),
            vmem((STAGES, RING, 2, 64, COLS), bf16),
            vmem((STAGES, RING, CORES, STAT, WIDTH), f32),
            vmem((STAGES, RING, CORES, STAT, WIDTH), bf16),
            vmem((STAGES, 2, STAT, WIDTH), bf16),
            vmem((STAGES, 2, STAT, WIDTH), bf16),
            vmem((CORES, STAGES, 2, STAT, WIDTH), bf16),
            vmem((STAGES, STAT, WIDTH), f32),
            dma((3,)), dma((STAGES,)), dma((STAGES,)), dma((STAGES,)), dma((3,)), dma((STAGES,)),
            dma((STAGES,)), dma((STAGES,)), dma((STAGES,)), dma((STAGES, CORES, 3)), dma((STAGES, CORES, 4, 3)),
            dma((STAGES, CORES, 3)), dma((4,)), dma((STAGES, 2)), dma((CORES, STAGES, 2)), dma((STAGES,)),
        ],
        compiler_params=pltpu.CompilerParams(
            collective_id=0, has_side_effects=True, vmem_limit_bytes=48 * 1024 * 1024
        ),
    )(spectra, bins, table)


def per_device(records, ref_bin, ref_table):
    spectra = records.reshape(STAT, 2, 16, 128).transpose(0, 2, 1, 3).reshape(STAT * 32, 128)
    args = (spectra, ref_bin.reshape(1024, 128), ref_table.T)
    out = exchange(*(pltpu.with_memory_space_constraint(arg, pltpu.HBM) for arg in args))
    return out.reshape(STAT, 16, 2, 128).transpose(0, 2, 1, 3).reshape(STAT, 2, 2048)


def solution(mesh):
    in_specs = (P(("grp", "sub"), None, None), P("grp", None, "sub", None), P())
    out_specs = P(("grp", "sub"), None, None)
    return jax.shard_map(
        per_device, mesh=mesh, in_specs=in_specs, out_specs=out_specs, check_vma=False
    )
```

time: 71.8 us -> 51.4 us (0.72)
  Pallas kernels: 65.5 us -> 50.4 us
  local copies, waits for them, and re-layouts: 4.42 us -> 0.8 us
  other arithmetic: 1.41 us -> 0 us
    pallas_call x1, Pallas kernels: 65.5 us -> 50.4 us  [exchange(): pl.pallas_call(kernel, out_shape=jax.ShapeDtypeStruct((STAT * 32, 128), f...]
    reshape x5 -> x0, local copies, waits for them, and re-layouts: 1.87 us -> none  [the longest x2 1.3 us: per_device(): out.reshape(BANDS, STAT, 2, HALF).transpose(1, 2, 0, 3)]
    convert_element_type x1 -> x0, other arithmetic: 1.4 us -> none  [per_device(): tile = ref_bin[0, :, 0, :].astype(jnp.bfloat16)]
    convert_element_type x4 -> x0, local copies, waits for them, and re-layouts: 1.04 us -> none  [per_device(): tile = ref_bin[0, :, 0, :].astype(jnp.bfloat16)]
where the time goes in v2:
time: 51.4 us; the launch traced here: 51.2 us
  Pallas kernels  50.4 us (98%)
  local copies, waits for them, and re-layouts  0.8 us (2%)
    pallas_call x1, Pallas kernels, exchange(): pl.pallas_call(kernel, out_shape=jax.ShapeDtypeStruct((STAT * 32, 128), f...  50.4 us

profile of v2, /device:TPU:1, one launch (start us, length us, event | category | flops | bytes accessed | tf_op | source)
XLA Modules:
  0.0 51.2 jit_solution(2987383574763541494)
XLA Ops:
  0.0 50.4 %shard_map.37 = f32[1024,128]{1,0:T(8,128)S(1)} custom-call(bf16[1024,128]{1,0:T(8,128)(2,1)} %bitcast.14, s32[1024,128]{1,0:T(8,128)} %bitcast.13, bf16[8,64]{1,0:T(8,128)(2,1)} %bitcast.15), custom_call_target="tpu_custom_call" | custom-call | tf_op jit(solution)/shard_map/pallas_call | solution.py:402
  50.4 0.8 %copy.7 = f32[32,2,2048]{2,1,0:T(2,128)} copy(f32[32,2,2048]{2,1,0:T(2,128)S(1)} %bitcast.12) | data formatting | bytes 1048576

commit v3 on v2

--- a/solution.py
+++ b/solution.py
@@ -92,19 +92,24 @@
                 xbuf[band, :, part * HALF + j * 128:part * HALF + (j + 1) * 128] = line.astype(bf16)
     pl.semaphore_wait(barrier, len(peers))
 
-    def first_hop(t):
+    def hop_p(t):
         here = slot(c, 0, 0)
         for index, sign in ((0, 1), (1, -1)):
             yy, zz = flow(c, sign, 0)
             for core in range(CORES):
                 start(xbuf.at[2 * core + t], ybuf.at[t, here], hop_send.at[t],
                       p_recv.at[t, c, index], device(x, yy, zz, core))
+
+    def hop_q(t):
+        here = slot(c, 0, 0)
         for index, sign in ((0, 1), (1, -1)):
             yy, zz = flow(c, 0, sign)
             for core in range(CORES):
                 start(xbuf.at[2 * core + t], ybuf.at[t, here], hop_send.at[t],
                       q_recv.at[t, c, 0, index], device(x, yy, zz, core))
-        start(xbuf.at[2 * other + t], ybuf.at[t, here], hop_send.at[t], own_recv.at[t],
+
+    def hop_x(t):
+        start(xbuf.at[2 * other + t], ybuf.at[t, slot(c, 0, 0)], hop_send.at[t], own_recv.at[t],
               device(x, y, z, other))
         for sign, index, row in ((1, 0, MINUS), (-1, 1, PLUS)):
             for core in range(CORES):
@@ -229,7 +234,7 @@
         loads[2].wait()
         table[1] = table[0]
 
-    def lookups(row):
+    def lookups(row, blocks=range(RING)):
         wide = jnp.concatenate([table[0], table[1]], axis=1).astype(f32)
         table_wide = wide
         names = []
@@ -240,7 +245,7 @@
         rx = wrap(x + ROW_SHIFT[row])
         rhi, rlo = lax.div(rx, 2), lax.rem(rx, 2)
         pieces = [d1buf[k, zz, rhi, rlo].astype(f32) for zz in range(RING) for k in range(CORES)]
-        for yy in range(RING):
+        for yy in blocks:
             mirrored = d2buf[:, yy, rhi, rlo].astype(f32).astype(jnp.int32).reshape(64, BLOCK)
             for side in range(2):
                 direct = jnp.concatenate(
@@ -250,8 +255,8 @@
                 for t in range(STAGES):
                     for part in range(2):
                         tab = names[2 * t + part]
-                        one = jnp.take_along_axis(tab, direct, axis=1)
-                        two = jnp.take_along_axis(tab, mirror, axis=1)
+                        one = jnp.take_along_axis(tab, direct, axis=1, mode="promise_in_bounds")
+                        two = jnp.take_along_axis(tab, mirror, axis=1, mode="promise_in_bounds")
                         value = one + two if part == 0 else one - two
                         dbuf[t, part, row, :, pl.ds(yy * BLOCK + side * 128, 128)] = value
 
@@ -321,41 +326,45 @@
         await_bytes(ybuf.at[t, pl.ds(0, 12)], q_send.at[t])
         await_bytes(ybuf.at[t, pl.ds(0, 12)], half_send.at[t])
 
-    first_hop(0)
-    first_hop(1)
+    hop_p(0)
+    hop_q(0)
+    hop_x(0)
     make_bins()
     send_bins()
+    hop_p(1)
+    hop_q(1)
+    hop_x(1)
     p_step(0)
     q_near(0)
     x_step(0)
     own_units(0)
-    q_step(0, 0)
+    q_step(0,0)
     p_step(1)
     x_step(1)
     own_units(1)
-    share_bins()
     p_last(0)
     x_last(0)
+    share_bins()
+    q_step(0,1)
+    q_step(0,2)
+    q_near(1)
+    q_step(1,0)
     wait_bins()
     lookups(0)
-    q_step(0, 1)
-    q_step(0, 2)
-    q_near(1)
     lookups(1)
-    q_step(1, 0)
-    q_step(0, 3)
+    q_step(0,3)
     p_last(1)
     lookups(2)
     lookups(3)
-    q_last(0, 0, 0)
-    corr(0, 0)
     x_last(1)
-    q_last(0, 0, 2)
-    corr(0, 1)
-    q_step(1, 1)
-    q_step(1, 2)
-    q_last(0, 0, 1)
-    corr(0, -1)
+    q_last(0,0,0)
+    corr(0,0)
+    q_last(0,0,2)
+    corr(0,1)
+    q_step(1,1)
+    q_step(1,2)
+    q_last(0,0,1)
+    corr(0,-1)
     q_last(0, 0, 3)
     for i in range(4):
         q_last(0, 1, i)
@@ -365,17 +374,17 @@
     sums_first(0)
     adjoint(0, 1)
     sums_second(0)
-    q_last(1, 0, 0)
-    corr(1, 0)
+    q_last(1,0,0)
+    corr(1,0)
+    q_last(1,0,2)
+    corr(1,1)
+    q_last(1,0,1)
+    corr(1,-1)
+    sums_forward(0)
     sends_done(0)
     for i in range(2):
         await_bytes(ybuf.at[0, pl.ds(0, 7), pl.ds(0, 16)], bin_send.at[i])
     await_bytes(ybuf.at[0, pl.ds(0, 8)], bin_send.at[2])
-    q_last(1, 0, 2)
-    corr(1, 1)
-    q_last(1, 0, 1)
-    corr(1, -1)
-    sums_forward(0)
     q_last(1, 0, 3)
     for i in range(4):
         q_last(1, 1, i)

time: 51.4 us -> 49.4 us (0.961)
  Pallas kernels: 50.4 us -> 48.5 us
    pallas_call x1, Pallas kernels: 50.4 us -> 48.5 us  [exchange(): pl.pallas_call(kernel, out_shape=jax.ShapeDtypeStruct((STAT * 32, 128), f...]
where the time goes in v3:
time: 49.4 us; the launch traced here: 49.3 us
  Pallas kernels  48.5 us (98%)
  local copies, waits for them, and re-layouts  0.8 us (2%)
    pallas_call x1, Pallas kernels, exchange(): pl.pallas_call(kernel, out_shape=jax.ShapeDtypeStruct((STAT * 32, 128), f...  48.5 us

profile of v3, /device:TPU:1, one launch (start us, length us, event | category | flops | bytes accessed | tf_op | source)
XLA Modules:
  0.0 49.3 jit_solution(4761598015150381695)
XLA Ops:
  0.0 48.5 %shard_map.37 = f32[1024,128]{1,0:T(8,128)S(1)} custom-call(bf16[1024,128]{1,0:T(8,128)(2,1)} %bitcast.14, s32[1024,128]{1,0:T(8,128)} %bitcast.13, bf16[8,64]{1,0:T(8,128)(2,1)} %bitcast.15), custom_call_target="tpu_custom_call" | custom-call | tf_op jit(solution)/shard_map/pallas_call | solution.py:411
  48.5 0.8 %copy.7 = f32[32,2,2048]{2,1,0:T(2,128)} copy(f32[32,2,2048]{2,1,0:T(2,128)S(1)} %bitcast.12) | data formatting | bytes 1048576

commit v4 on v3

--- a/solution.py
+++ b/solution.py
@@ -20,6 +20,7 @@
 MESH = pl.DeviceIdType.MESH
 OPP, PLUS, MINUS, OWN = 0, 1, 2, 3
 ROW_SHIFT = (2, 1, 3, 0)
+DIRECT = (0, 1)
 
 
 def wrap(value):
@@ -150,8 +151,13 @@
 
     def p_last(t):
         for k in range(CORES):
-            await_bytes(ybuf.at[t, slot(k, 2, 0)], p_recv.at[t, k, 2])
+            here = slot(k, 2, 0)
+            await_bytes(ybuf.at[t, here], p_recv.at[t, k, 2])
             q_out(t, k, 3)
+            if t in DIRECT:
+                yy, zz = flow(k, 0, 2)
+                start(ybuf.at[t, here], ybuf.at[t, here], q_send.at[t], q_recv.at[t, k, 3, 2],
+                      device(x, yy, zz, c))
 
     def x_step(t):
         for row, index, sign in ((MINUS, 0, 1), (PLUS, 1, -1)):
@@ -175,6 +181,8 @@
             for k in range(CORES):
                 here = slot(k, p, sign)
                 await_bytes(ybuf.at[t, here], q_recv.at[t, k, p_index, index])
+                if p_index == 3 and t in DIRECT:
+                    continue
                 yy, zz = flow(k, 0, -sign)
                 part = pl.ds(16 * index, 16)
                 start(ybuf.at[t, here, part], ybuf.at[t, here, part], half_send.at[t],
@@ -273,45 +281,44 @@
             value = got.reshape(RING, 64, BLOCK) * scale - dbuf[t, part, :, :, pl.ds(base, BLOCK)]
             sbuf[t, :, part, :, pl.ds(base, BLOCK)] = value.astype(bf16)
 
-    def adjoint(t, half):
-        left = sbuf[t, 2 * half:2 * half + 2].reshape(ROWS, COLS)
-        for j in range(2):
-            real = ybuf[t, :, :, j * 256:(j + 1) * 256].reshape(COLS, 256)
-            imag = ybuf[t, :, :, HALF + j * 256:HALF + (j + 1) * 256].reshape(COLS, 256)
-            a = jnp.dot(left, real, preferred_element_type=f32).reshape(2, 2, 64, 256)
-            b = jnp.dot(left, imag, preferred_element_type=f32).reshape(2, 2, 64, 256)
-            re = (a[:, 0] - b[:, 1]).reshape(2, CORES, STAT, 256)
-            im = (b[:, 0] + a[:, 1]).reshape(2, CORES, STAT, 256)
-            for value, base in ((re, j * 256), (im, HALF + j * 256)):
-                pbuf[t, 2 * half:2 * half + 2, :, :, base:base + 256] = value
-                hbuf[t, 2 * half:2 * half + 2, :, :, base:base + 256] = value.astype(bf16)
-
-    def sums_first(t):
+    def adjoint(t, half, j):
+        rows = slice(2 * half, 2 * half + 2)
+        left = sbuf[t, rows].reshape(ROWS, COLS)
+        real = ybuf[t, :, :, j * 256:(j + 1) * 256].reshape(COLS, 256)
+        imag = ybuf[t, :, :, HALF + j * 256:HALF + (j + 1) * 256].reshape(COLS, 256)
+        a = jnp.dot(left, real, preferred_element_type=f32).reshape(2, 2, 64, 256)
+        b = jnp.dot(left, imag, preferred_element_type=f32).reshape(2, 2, 64, 256)
+        re = (a[:, 0] - b[:, 1]).reshape(2, CORES, STAT, 256)
+        im = (b[:, 0] + a[:, 1]).reshape(2, CORES, STAT, 256)
+        for value, cols in ((re, slice(0, 256)), (im, slice(256, HALF))):
+            pbuf[t, rows, :, j, :, cols] = value
+            hbuf[t, rows, :, j, :, cols] = value.astype(bf16)
+
+    def sums_first(t, j):
+        for k, to in ((0, wrap(x + 1)), (1, wrap(x - 1))):
+            start(hbuf.at[t, OPP, k, j], rs1.at[t, k, j], rs_send.at[t], rs_recv.at[t, k, j],
+                  device(to, y, z, c))
+
+    def sums_second(t):
         up, down = wrap(x + 1), wrap(x - 1)
-        start(hbuf.at[t, OPP, 0], rs1.at[t, 0], rs_send.at[t], rs_recv.at[t, 0], device(up, y, z, c))
-        start(hbuf.at[t, OPP, 1], rs1.at[t, 1], rs_send.at[t], rs_recv.at[t, 1], device(down, y, z, c))
         start(hbuf.at[t, PLUS, 1], fbuf.at[c, t, 0], rs_send.at[t], f_recv.at[c, t, 0], device(up, y, z, 1))
-
-    def sums_second(t):
-        down = wrap(x - 1)
         start(hbuf.at[t, MINUS, 0], fbuf.at[c, t, 1], rs_send.at[t], f_recv.at[c, t, 1], device(down, y, z, 0))
         start(pbuf.at[t, OWN, other], nbuf.at[t], own_send.at[t], n_recv.at[t], device(x, y, z, other))
 
     def sums_forward(t):
-        await_bytes(rs1.at[t, 0], rs_recv.at[t, 0])
-        gbuf[t, 0] = (rs1[t, 0].astype(f32) + pbuf[t, PLUS, 0]).astype(bf16)
-        start(gbuf.at[t, 0], fbuf.at[c, t, 0], fin_send.at[t], f_recv.at[c, t, 0],
-              device(wrap(x + 1), y, z, 0))
-        await_bytes(rs1.at[t, 1], rs_recv.at[t, 1])
-        gbuf[t, 1] = (rs1[t, 1].astype(f32) + pbuf[t, MINUS, 1]).astype(bf16)
-        start(gbuf.at[t, 1], fbuf.at[c, t, 1], fin_send.at[t], f_recv.at[c, t, 1],
-              device(wrap(x - 1), y, z, 1))
+        for j in range(2):
+            for k, row, to in ((0, PLUS, wrap(x + 1)), (1, MINUS, wrap(x - 1))):
+                await_bytes(rs1.at[t, k, j], rs_recv.at[t, k, j])
+                gbuf[t, k, j] = (rs1[t, k, j].astype(f32) + pbuf[t, row, k, j]).astype(bf16)
+                start(gbuf.at[t, k, j], fbuf.at[c, t, k, j], fin_send.at[t], f_recv.at[c, t, k],
+                      device(to, y, z, k))
 
     def store(band, value):
         value = value * (1.0 / math.sqrt(COLS * RING))
         for part in range(2):
             for j in range(4):
-                piece = value[:, part * HALF + j * 128:part * HALF + (j + 1) * 128]
+                at = part * 256 + (j % 2) * 128
+                piece = value[j // 2, :, at:at + 128]
                 out_ref[pl.ds(band * 8 + j * 2 + part, STAT, stride=32), :] = piece
 
     def sums_last(t):
@@ -323,8 +330,9 @@
 
     def sends_done(t):
         await_bytes(ybuf.at[t, pl.ds(0, 13)], hop_send.at[t])
-        await_bytes(ybuf.at[t, pl.ds(0, 12)], q_send.at[t])
-        await_bytes(ybuf.at[t, pl.ds(0, 12)], half_send.at[t])
+        straight = 2 if t in DIRECT else 0
+        await_bytes(ybuf.at[t, pl.ds(0, 12 + straight)], q_send.at[t])
+        await_bytes(ybuf.at[t, pl.ds(0, 12 - straight)], half_send.at[t])
 
     hop_p(0)
     hop_q(0)
@@ -350,32 +358,39 @@
     q_near(1)
     q_step(1,0)
     wait_bins()
-    lookups(0)
-    lookups(1)
+    lookups(0, range(0, 2))
+    lookups(0, range(2, 4))
+    lookups(1, range(0, 2))
     q_step(0,3)
+    lookups(1, range(2, 4))
     p_last(1)
-    lookups(2)
-    lookups(3)
+    lookups(2, range(0, 2))
+    lookups(2, range(2, 4))
     x_last(1)
+    q_step(1,1)
+    lookups(3, range(0, 2))
+    lookups(3, range(2, 4))
+    q_step(1,2)
     q_last(0,0,0)
     corr(0,0)
     q_last(0,0,2)
     corr(0,1)
-    q_step(1,1)
-    q_step(1,2)
     q_last(0,0,1)
     corr(0,-1)
     q_last(0, 0, 3)
     for i in range(4):
         q_last(0, 1, i)
     corr(0, 2)
-    q_step(1, 3)
-    adjoint(0, 0)
-    sums_first(0)
-    adjoint(0, 1)
+    adjoint(0, 0, 0)
+    sums_first(0, 0)
+    adjoint(0, 0, 1)
+    sums_first(0, 1)
+    adjoint(0, 1, 0)
+    adjoint(0, 1, 1)
     sums_second(0)
     q_last(1,0,0)
     corr(1,0)
+    q_step(1, 3)
     q_last(1,0,2)
     corr(1,1)
     q_last(1,0,1)
@@ -389,9 +404,12 @@
     for i in range(4):
         q_last(1, 1, i)
     corr(1, 2)
-    adjoint(1, 0)
-    sums_first(1)
-    adjoint(1, 1)
+    adjoint(1, 0, 0)
+    sums_first(1, 0)
+    adjoint(1, 0, 1)
+    sums_first(1, 1)
+    adjoint(1, 1, 0)
+    adjoint(1, 1, 1)
     sums_second(1)
     sums_last(0)
     sums_forward(1)
@@ -427,15 +445,15 @@
             vmem((CORES, RING, 2, 2, STAT, BLOCK), bf16),
             vmem((STAGES, 2, RING, 64, COLS), f32),
             vmem((STAGES, RING, 2, 64, COLS), bf16),
-            vmem((STAGES, RING, CORES, STAT, WIDTH), f32),
-            vmem((STAGES, RING, CORES, STAT, WIDTH), bf16),
-            vmem((STAGES, 2, STAT, WIDTH), bf16),
-            vmem((STAGES, 2, STAT, WIDTH), bf16),
-            vmem((CORES, STAGES, 2, STAT, WIDTH), bf16),
-            vmem((STAGES, STAT, WIDTH), f32),
+            vmem((STAGES, RING, CORES, 2, STAT, HALF), f32),
+            vmem((STAGES, RING, CORES, 2, STAT, HALF), bf16),
+            vmem((STAGES, 2, 2, STAT, HALF), bf16),
+            vmem((STAGES, 2, 2, STAT, HALF), bf16),
+            vmem((CORES, STAGES, 2, 2, STAT, HALF), bf16),
+            vmem((STAGES, 2, STAT, HALF), f32),
             dma((3,)), dma((STAGES,)), dma((STAGES,)), dma((STAGES,)), dma((3,)), dma((STAGES,)),
             dma((STAGES,)), dma((STAGES,)), dma((STAGES,)), dma((STAGES, CORES, 3)), dma((STAGES, CORES, 4, 3)),
-            dma((STAGES, CORES, 3)), dma((4,)), dma((STAGES, 2)), dma((CORES, STAGES, 2)), dma((STAGES,)),
+            dma((STAGES, CORES, 3)), dma((4,)), dma((STAGES, 2, 2)), dma((CORES, STAGES, 2)), dma((STAGES,)),
         ],
         compiler_params=pltpu.CompilerParams(
             collective_id=0, has_side_effects=True, vmem_limit_bytes=48 * 1024 * 1024

time: 49.4 us -> 49.1 us (level)
  no operation moved by 1% of the time
where the time goes in v4:
time: 49.1 us; the launch traced here: 48.9 us
  Pallas kernels  48.1 us (98%)
  local copies, waits for them, and re-layouts  0.8 us (2%)
    pallas_call x1, Pallas kernels, exchange(): pl.pallas_call(kernel, out_shape=jax.ShapeDtypeStruct((STAT * 32, 128), f...  48.1 us

profile of v4, /device:TPU:1, one launch (start us, length us, event | category | flops | bytes accessed | tf_op | source)
XLA Modules:
  0.0 48.9 jit_solution(9532936969099210283)
XLA Ops:
  0.0 48.1 %shard_map.37 = f32[1024,128]{1,0:T(8,128)S(1)} custom-call(bf16[1024,128]{1,0:T(8,128)(2,1)} %bitcast.14, s32[1024,128]{1,0:T(8,128)} %bitcast.13, bf16[8,64]{1,0:T(8,128)(2,1)} %bitcast.15), custom_call_target="tpu_custom_call" | custom-call | tf_op jit(solution)/shard_map/pallas_call | solution.py:429
  48.1 0.8 %copy.7 = f32[32,2,2048]{2,1,0:T(2,128)} copy(f32[32,2,2048]{2,1,0:T(2,128)S(1)} %bitcast.12) | data formatting | bytes 1048576

commit v5 on v4

--- a/solution.py
+++ b/solution.py
@@ -353,9 +353,9 @@
     p_last(0)
     x_last(0)
     share_bins()
+    q_near(1)
     q_step(0,1)
     q_step(0,2)
-    q_near(1)
     q_step(1,0)
     wait_bins()
     lookups(0, range(0, 2))

time: 49.1 us -> 49.1 us (level)
  no operation moved by 1% of the time
where the time goes in v5:
time: 49.1 us; the launch traced here: 49 us
  Pallas kernels  48.2 us (98%)
  local copies, waits for them, and re-layouts  0.8 us (2%)
    pallas_call x1, Pallas kernels, exchange(): pl.pallas_call(kernel, out_shape=jax.ShapeDtypeStruct((STAT * 32, 128), f...  48.2 us

profile of v5, /device:TPU:1, one launch (start us, length us, event | category | flops | bytes accessed | tf_op | source)
XLA Modules:
  0.0 49.0 jit_solution(2174707343481169230)
XLA Ops:
  0.0 48.2 %shard_map.37 = f32[1024,128]{1,0:T(8,128)S(1)} custom-call(bf16[1024,128]{1,0:T(8,128)(2,1)} %bitcast.14, s32[1024,128]{1,0:T(8,128)} %bitcast.13, bf16[8,64]{1,0:T(8,128)(2,1)} %bitcast.15), custom_call_target="tpu_custom_call" | custom-call | tf_op jit(solution)/shard_map/pallas_call | solution.py:429
  48.2 0.8 %copy.7 = f32[32,2,2048]{2,1,0:T(2,128)} copy(f32[32,2,2048]{2,1,0:T(2,128)S(1)} %bitcast.12) | data formatting | bytes 1048576
